TPU v7x, 32 devices: a whole 2x2x4 slice. The times are simulated.
32 devices in a mesh: dp: 4 (over y, x), expert: 8 (over z, core).
Axes of the slice: x: 2, y: 2, z: 4, core: 2. Of those that a mesh axis runs over, the one named last changes fastest.
Arguments:
- tokens: bfloat16 [4096, 2048], P(('dp', 'expert')), may hold values from -6 to 6
- cotangent: bfloat16 [4096, 2048], P(('dp', 'expert')), may hold values from -6 to 6
- routes: int32 [4096, 2], P(('dp', 'expert')), may hold values from 0 to 7, as said below
- route_weights: float32 [4096, 2], P(('dp', 'expert')), may hold values from 0.1 to 1
- capacity: int32 [8], replicated, may hold values from 16 to 32, as said below
- w_in: bfloat16 [8, 2, 1408, 2048], P('expert', None, 'dp'), may hold values from -0.125 to 0.125
- w_down: bfloat16 [8, 1408, 2048], P('expert', 'dp'), may hold values from -0.15625 to 0.15625
Outputs:
- mixed: bfloat16 [4096, 2048], P(('dp', 'expert'))
- d_tokens: bfloat16 [4096, 2048], P(('dp', 'expert'))
- d_route_weights: float32 [4096, 2], P(('dp', 'expert'))
- d_w_in: bfloat16 [8, 2, 1408, 2048], P('expert', None, 'dp')
- d_w_down: bfloat16 [8, 1408, 2048], P('expert', 'dp')
Inputs may be any that keep to these rules, and one draw needn't show every extreme that they name: Each token names two different experts; in every block of 128 rows (one device's tokens) some expert whose capacity is 32 is named by 32 or more routes. Some expert has capacity 32.
All inputs are finite; a program needn't handle non-finite values.
Results may differ from a plain program's by a relative error of at most 0.013.
Values may be sent and summed in bfloat16 or wider, within the bound.
A program may use at most 128 MiB of HBM per device.

v0:
```python
import jax
import jax.numpy as jnp
from jax import lax
from jax.sharding import PartitionSpec as P


def expert_forward(inputs, weights_in, weights_down):
    gate_value = jnp.einsum(
        "gecd,ehd->gech", inputs, weights_in[:, 0], preferred_element_type=jnp.float32
    )
    up_value = jnp.einsum(
        "gecd,ehd->gech", inputs, weights_in[:, 1], preferred_element_type=jnp.float32
    )
    sig_gate = jax.nn.sigmoid(gate_value)
    act_gate = gate_value * sig_gate
    hidden = (act_gate * up_value).astype(jnp.bfloat16)
    partial_out = jnp.einsum(
        "gech,ehd->gecd", hidden, weights_down, preferred_element_type=jnp.float32
    )
    return ((gate_value, up_value, sig_gate, act_gate, hidden), partial_out)


def expert_backward(inputs, scaled, weights_in, weights_down, saved):
    gate_value, up_value, sig_gate, act_gate, hidden = saved
    hidden_grad = jnp.einsum(
        "gecd,ehd->gech", scaled, weights_down, preferred_element_type=jnp.float32
    )
    slope_gate = sig_gate * (1.0 + gate_value * (1.0 - sig_gate))
    gate_grad = (hidden_grad * up_value * slope_gate).astype(jnp.bfloat16)
    up_grad = (hidden_grad * act_gate).astype(jnp.bfloat16)
    gate_weight_grad = jnp.einsum(
        "gech,gecd->ehd", gate_grad, inputs, preferred_element_type=jnp.float32
    )
    up_weight_grad = jnp.einsum(
        "gech,gecd->ehd", up_grad, inputs, preferred_element_type=jnp.float32
    )
    down_weight_grad = jnp.einsum(
        "gech,gecd->ehd", hidden, scaled, preferred_element_type=jnp.float32
    )
    input_grad = jnp.einsum(
        "gech,ehd->gecd", gate_grad, weights_in[:, 0], preferred_element_type=jnp.float32
    )
    input_grad = input_grad + jnp.einsum(
        "gech,ehd->gecd", up_grad, weights_in[:, 1], preferred_element_type=jnp.float32
    )
    return (jnp.stack([gate_weight_grad, up_weight_grad], axis=1), down_weight_grad, input_grad)


def body(tokens, cotangent, routes, route_weights, capacity, w_in, w_down):
    experts = capacity.shape[0]
    expert_devs = lax.axis_size("expert")
    local_experts = experts // expert_devs
    tok_rows = tokens.shape[0]
    width = tokens.shape[1]
    slots = tok_rows * 2 // experts
    flat_expert = routes.reshape(-1)
    expert_ids = jnp.arange(experts, dtype=jnp.int32)
    onehot = (flat_expert[:, None] == expert_ids[None, :]).astype(jnp.int32)
    earlier = jnp.cumsum(onehot, axis=0) - onehot
    route_rank = jnp.sum(earlier * onehot, axis=1)
    cap_limit = jnp.sum(onehot * capacity[None, :], axis=1)
    kept_mask = route_rank < cap_limit
    dummy = experts * slots
    slot_target = jnp.where(kept_mask, flat_expert * slots + route_rank, dummy)
    route_count = 2 * tok_rows
    route_ids = jnp.arange(route_count, dtype=jnp.int32)
    slot_owner = (
        jnp.full((dummy + 1,), route_count, jnp.int32).at[slot_target].set(route_ids)[:dummy]
    )
    token_of = slot_owner // 2
    padded_tokens = jnp.concatenate([tokens, jnp.zeros((1, width), tokens.dtype)], axis=0)
    padded_cot = jnp.concatenate([cotangent, jnp.zeros((1, width), cotangent.dtype)], axis=0)
    padded_weights = jnp.concatenate(
        [route_weights.reshape(-1), jnp.zeros((1,), jnp.float32)], axis=0
    )
    bucket_shape = (expert_devs, local_experts, slots, width)
    send_inputs = padded_tokens[token_of].reshape(bucket_shape)
    send_scaled = (
        (padded_weights[slot_owner][:, None] * padded_cot[token_of].astype(jnp.float32))
        .astype(jnp.bfloat16)
        .reshape(bucket_shape)
    )
    recv_inputs = lax.all_to_all(send_inputs, "expert", split_axis=0, concat_axis=0, tiled=True)
    use_inputs = lax.all_gather(recv_inputs, "dp", axis=0, tiled=True)
    saved, partial_out = expert_forward(use_inputs, w_in, w_down)
    out_local = lax.psum_scatter(
        partial_out.astype(jnp.bfloat16), "dp", scatter_dimension=0, tiled=True
    )
    out_back = lax.all_to_all(out_local, "expert", split_axis=0, concat_axis=0, tiled=True)
    recv_scaled = lax.all_to_all(send_scaled, "expert", split_axis=0, concat_axis=0, tiled=True)
    use_scaled = lax.all_gather(recv_scaled, "dp", axis=0, tiled=True)
    in_weight_grad, down_weight_grad, input_grad = expert_backward(
        use_inputs, use_scaled, w_in, w_down, saved
    )
    grad_local = lax.psum_scatter(
        input_grad.astype(jnp.bfloat16), "dp", scatter_dimension=0, tiled=True
    )
    grad_back = lax.all_to_all(grad_local, "expert", split_axis=0, concat_axis=0, tiled=True)
    flat_out = jnp.concatenate(
        [out_back.reshape(dummy, width), jnp.zeros((1, width), jnp.bfloat16)], axis=0
    )
    flat_grad = jnp.concatenate(
        [grad_back.reshape(dummy, width), jnp.zeros((1, width), jnp.bfloat16)], axis=0
    )
    out_route = flat_out[slot_target].reshape(tok_rows, 2, width).astype(jnp.float32)
    grad_route = flat_grad[slot_target].reshape(tok_rows, 2, width).astype(jnp.float32)
    mixed = jnp.sum(route_weights[:, :, None] * out_route, axis=1).astype(jnp.bfloat16)
    d_route_weights = jnp.sum(out_route * cotangent.astype(jnp.float32)[:, None, :], axis=2)
    d_tokens = jnp.sum(grad_route, axis=1).astype(jnp.bfloat16)
    return (
        mixed,
        d_tokens,
        d_route_weights,
        in_weight_grad.astype(jnp.bfloat16),
        down_weight_grad.astype(jnp.bfloat16),
    )


def solution(mesh):
    placed = (
        P(("dp", "expert"), None),
        P(("dp", "expert"), None),
        P(("dp", "expert"), None),
        P(("dp", "expert"), None),
        P(),
        P("expert", None, "dp", None),
        P("expert", "dp", None),
    )
    return jax.shard_map(
        body,
        mesh=mesh,
        in_specs=placed,
        out_specs=(
            P(("dp", "expert"), None),
            P(("dp", "expert"), None),
            P(("dp", "expert"), None),
            P("expert", None, "dp", None),
            P("expert", "dp", None),
        ),
        check_vma=False,
    )
```

profile of v0, /device:TPU:0, one launch (start us, length us, event | category | flops | bytes accessed | tf_op | source)
XLA Modules:
  0.0 320.7 jit_solution(16261280849117789705)
XLA Ops:
  14.9 32.8 %all_to_all.20 = bf16[8,1,32,2048]{3,2,1,0:T(8,128)(2,1)} all-to-all(bf16[8,1,32,2048]{3,2,1,0:T(8,128)(2,1)S(1)} %bitcast.184), channel_id=1, replica_groups=mesh['dp'=4,'expert'=8] {'expert'}, dimensions={0} | all-to-all | bytes 2097152 | tf_op jit(solution)/shard_map/all_to_all | solution.py:83
  51.8 29.7 %all_to_all.21 = bf16[8,1,32,2048]{3,2,1,0:T(8,128)(2,1)} all-to-all(bf16[8,1,32,2048]{3,2,1,0:T(8,128)(2,1)S(1)} %fusion.40), channel_id=1, replica_groups=mesh['dp'=4,'expert'=8] {'expert'}, dimensions={0} | all-to-all | bytes 2097152 | tf_op jit(solution)/shard_map/all_to_all | solution.py:90
  81.5 18.0 %all-gather.3.cloned.1.call-done = bf16[32,1,32,2048]{3,2,1,0:T(8,128)(2,1)} async-done(((bf16[8,1,32,2048]{3,2,1,0:T(8,128)(2,1)}), bf16[32,1,32,2048]{3,2,1,0:T(8,128)(2,1)}) %all-gather.3.cloned.1.call-update) | async-done | bytes 4194320 | tf_op jit(solution)/shard_map/all_gather | solution.py:84
  99.5 6.3 %fusion.8 = f32[32,32,352]{2,1,0:T(8,128)} fusion(bf16[32,1,32,2048]{3,2,1,0:T(8,128)(2,1)} %all-gather.3.cloned.1.call-done, bf16[1,2,352,2048]{3,2,1,0:T(8,128)(2,1)} %param.12), kind=kOutput, calls=%fused_computation.15 | convolution fusion | flops 1476395008 | bytes 7077888 | tf_op jit(solution)/shard_map/gecd,ehd->gech/dot_general | solution.py:11
  105.8 3.5 %fusion.10 = f32[32,32,352]{2,1,0:T(8,128)} fusion(bf16[32,1,32,2048]{3,2,1,0:T(8,128)(2,1)S(1)} %copy-done.10, bf16[1,2,352,2048]{3,2,1,0:T(8,128)(2,1)S(1)} %copy-done.2), kind=kOutput, calls=%fused_computation.17 | convolution fusion | flops 1476395008 | bytes 7077888 | tf_op jit(solution)/shard_map/gecd,ehd->gech/dot_general | solution.py:8
  109.3 44.7 %all-gather.5.cloned.1.call-done = bf16[32,1,32,2048]{3,2,1,0:T(8,128)(2,1)} async-done(((bf16[8,1,32,2048]{3,2,1,0:T(8,128)(2,1)}), bf16[32,1,32,2048]{3,2,1,0:T(8,128)(2,1)}) %all-gather.5.cloned.1.call-update) | async-done | bytes 4194320 | tf_op jit(solution)/shard_map/all_gather | solution.py:91
  154.1 5.9 %fusion.62 = (bf16[32,32,352]{2,1,0:T(8,128)(2,1)S(1)}, bf16[32,1,32,352]{3,2,0,1:T(8,128)(2,1)S(1)}, bf16[32,32,352]{2,1,0:T(8,128)(2,1)S(1)}) fusion(f32[32,32,352]{2,1,0:T(8,128)} %fusion.10, f32[32,32,352]{2,1,0:T(8,128)} %fusion.8, bf16[1,352,2048]{2,1,0:T(8,128)(2,1)S(1)} %copy-done, bf16[32,1,32,2048]{3,2,1,0:T(8,128)(2,1)} %all-gather.5.cloned.1.call-done), kind=kOutput, calls=%fused_computation.62 | convolution fusion | flops 1481801728 | bytes 10682368 | tf_op jit(solution)/shard_map/gecd,ehd->gech/dot_general | solution.py:25
  160.9 4.3 %convert_bitcast_fusion = bf16[32,1,32,2048]{3,2,0,1:T(8,128)(2,1)} fusion(bf16[32,32,352]{2,1,0:T(8,128)(2,1)S(1)} %get-tuple-element.16, bf16[1,352,2048]{2,1,0:T(8,128)(2,1)S(1)} %copy-done), kind=kOutput, calls=%fused_computation.19 | convolution fusion | flops 1478492160 | bytes 6356992 | tf_op jit(solution)/shard_map/gech,ehd->gecd/dot_general | solution.py:17
  165.4 3.8 %fusion.52 = f32[32,32,2048]{2,1,0:T(8,128)S(1)} fusion(bf16[1,2,352,2048]{3,2,1,0:T(8,128)(2,1)} %param.12, bf16[32,1,32,352]{3,2,0,1:T(8,128)(2,1)S(1)} %get-tuple-element.15), kind=kOutput, calls=%fused_computation.52 | convolution fusion | flops 1476395008 | bytes 10551296 | tf_op jit(solution)/shard_map/gech,ehd->gecd/dot_general | solution.py:40
  169.3 4.3 %fusion.12 = bf16[32,1,32,2048]{3,2,0,1:T(8,128)(2,1)} fusion(f32[32,32,2048]{2,1,0:T(8,128)S(1)} %fusion.52, bf16[32,32,352]{2,1,0:T(8,128)(2,1)S(1)} %get-tuple-element.14, bf16[1,2,352,2048]{3,2,1,0:T(8,128)(2,1)S(1)} %copy-done.3), kind=kOutput, calls=%fused_computation.20 | convolution fusion | flops 1480589312 | bytes 14811136 | tf_op jit(solution)/shard_map/gech,ehd->gecd/dot_general | solution.py:43
  175.8 42.2 %reduce-scatter.3.cloned.1.call-done = bf16[8,1,32,2048]{3,2,0,1:T(8,128)(2,1)} async-done(((bf16[32,1,32,2048]{3,2,0,1:T(8,128)(2,1)}), bf16[8,1,32,2048]{3,2,0,1:T(8,128)(2,1)}) %reduce-scatter.3.cloned.1.call-update) | async-done | bytes 1048592 | tf_op jit(solution)/shard_map/reduce_scatter | solution.py:86
  218.0 4.6 %all-to-all-start.1 = ((bf16[8,1,32,2048]{3,2,1,0:T(8,128)(2,1)}), bf16[8,1,32,2048]{3,2,1,0:T(8,128)(2,1)S(1)}, u32[]{:S(2)}, u32[]{:S(2)}) async-start(bf16[8,1,32,2048]{3,2,1,0:T(8,128)(2,1)} %bitcast.187), calls=%async_computation.2 | async-start | bytes 2097152 | tf_op jit(solution)/shard_map/all_to_all | solution.py:89
  222.7 5.1 %fusion.34 = bf16[1,1,352,2048]{3,2,1,0:T(8,128)(2,1)} fusion(bf16[32,32,352]{2,1,0:T(8,128)(2,1)S(1)} %get-tuple-element.14, bf16[32,1,32,2048]{3,2,1,0:T(8,128)(2,1)} %all-gather.3.cloned.1.call-done), kind=kOutput, calls=%fused_computation.29 | convolution fusion | flops 1477115904 | bytes 6356992 | tf_op jit(solution)/shard_map/gech,gecd->ehd/dot_general | solution.py:34
  227.8 2.8 fusion.31
  230.6 43.2 %reduce-scatter.5.cloned.1.call-done = bf16[8,1,32,2048]{3,2,0,1:T(8,128)(2,1)} async-done(((bf16[32,1,32,2048]{3,2,0,1:T(8,128)(2,1)}), bf16[8,1,32,2048]{3,2,0,1:T(8,128)(2,1)}) %reduce-scatter.5.cloned.1.call-update) | async-done | bytes 1048592 | tf_op jit(solution)/shard_map/reduce_scatter | solution.py:95
  273.9 4.6 %all-to-all-start.3 = ((bf16[8,1,32,2048]{3,2,1,0:T(8,128)(2,1)}), bf16[8,1,32,2048]{3,2,1,0:T(8,128)(2,1)}, u32[]{:S(2)}, u32[]{:S(2)}) async-start(bf16[8,1,32,2048]{3,2,1,0:T(8,128)(2,1)} %bitcast.186), calls=%async_computation.5 | async-start | bytes 2097152 | tf_op jit(solution)/shard_map/all_to_all | solution.py:98
  278.5 3.8 %pad_maximum_fusion = bf16[1,2,352,2048]{3,2,1,0:T(8,128)(2,1)} fusion(bf16[1,1,352,2048]{3,2,1,0:T(8,128)(2,1)} %fusion.34, bf16[1,1,352,2048]{3,2,1,0:T(8,128)(2,1)} %fusion.31), kind=kLoop, calls=%fused_computation.24 | loop fusion | flops 1441792 | bytes 5767168 | tf_op jit(solution)/shard_map/stack | solution.py:46
  282.3 2.8 fusion.37
  286.4 2.3 gather_fusion.1
  288.7 2.4 reshape.229
  291.1 6.0 %multiply_reduce_fusion = (f32[128,2]{1,0:T(8,128)}, bf16[128,2048]{1,0:T(8,128)(2,1)}) fusion(f32[128,2,2048]{2,1,0:T(2,128)S(1)} %reshape.229, f32[128,2048]{1,0:T(8,128)} %convert_element_type.115, f32[128,2]{1,0:T(8,128)} %copy-done.8), kind=kLoop, calls=%fused_computation.33 | loop fusion | flops 1834752 | bytes 3672064 | tf_op jit(solution)/shard_map/reduce_sum | solution.py:108
  298.5 6.7 %all-to-all-done.3 = bf16[8,1,32,2048]{3,2,1,0:T(8,128)(2,1)} async-done(((bf16[8,1,32,2048]{3,2,1,0:T(8,128)(2,1)}), bf16[8,1,32,2048]{3,2,1,0:T(8,128)(2,1)}, u32[]{:S(2)}, u32[]{:S(2)}) %all-to-all-start.3) | async-done | bytes 1048608 | tf_op jit(solution)/shard_map/all_to_all | solution.py:98
  306.5 2.3 gather_fusion.4
  310.5 3.6 %reduce_sum.57 = bf16[128,2048]{1,0:T(8,128)(2,1)} reduce(bf16[128,2,2048]{2,1,0:T(2,128)(2,1)S(1)} %reshape.228, bf16[]{:T(256)} %constant.14.clone.1), dimensions={1}, to_apply=%region_8.9 | reduce | flops 262144 | bytes 1572866 | tf_op jit(solution)/shard_map/reduce_sum | solution.py:109
  (72 shorter events, 20.8 us)
Async XLA Ops:
  7.2 146.9 %copy-start = (bf16[1,352,2048]{2,1,0:T(8,128)(2,1)S(1)}, bf16[1,352,2048]{2,1,0:T(8,128)(2,1)}, u32[]{:S(2)}) copy-start(bf16[1,352,2048]{2,1,0:T(8,128)(2,1)} %param.13) | copy-start | bytes 4325380
  7.2 92.3 %all-gather.3.cloned.1.call-start = ((), (), s32[]{:S(2)}) async-start(), calls=%async_computation.6 | async-start | bytes 5242880 | tf_op jit(solution)/shard_map/all_gather | solution.py:84
  14.9 32.9 %copy-start.9 = (f32[128,2]{0,1:T(2,128)S(1)}, f32[128,2]{0,1:T(2,128)}, u32[]{:S(2)}) copy-start(f32[128,2]{0,1:T(2,128)} %param.10) | copy-start | bytes 3076
  47.7 2.4 copy-start.4
  47.7 106.3 %all-gather.5.cloned.1.call-start = ((), (), s32[]{:S(2)}) async-start(), calls=%async_computation.8 | async-start | bytes 5242880 | tf_op jit(solution)/shard_map/all_gather | solution.py:91
  47.9 2.2 copy-start.8
  81.5 136.5 %reduce-scatter.3.cloned.1.call-start = ((), (), s32[]{:S(2)}) async-start(), calls=%async_computation.7 | async-start | bytes 5242880 | tf_op jit(solution)/shard_map/reduce_scatter | solution.py:86
  99.5 6.3 %copy-start.2 = (bf16[1,2,352,2048]{3,2,1,0:T(8,128)(2,1)S(1)}, bf16[1,2,352,2048]{3,2,1,0:T(8,128)(2,1)}, u32[]{:S(2)}) copy-start(bf16[1,2,352,2048]{3,2,1,0:T(8,128)(2,1)} %param.12) | copy-start | bytes 8650756
  99.5 6.3 %copy-start.10 = (bf16[32,1,32,2048]{3,2,1,0:T(8,128)(2,1)S(1)}, bf16[32,1,32,2048]{3,2,1,0:T(8,128)(2,1)}, u32[]{:S(2)}) copy-start(bf16[32,1,32,2048]{3,2,1,0:T(8,128)(2,1)} %all-gather.3.cloned.1.call-done) | copy-start | bytes 12582916
  160.0 0.9 copy-start.13
  160.0 5.4 %copy-start.6 = (bf16[32,1,32,352]{3,2,0,1:T(8,128)(2,1)}, bf16[32,1,32,352]{3,2,0,1:T(8,128)(2,1)S(1)}, u32[]{:S(2)}) copy-start(bf16[32,1,32,352]{3,2,0,1:T(8,128)(2,1)S(1)} %get-tuple-element.15) | copy-start | bytes 2162692
  165.2 108.7 %reduce-scatter.5.cloned.1.call-start = ((), (), s32[]{:S(2)}) async-start(), calls=%async_computation.9 | async-start | bytes 5242880 | tf_op jit(solution)/shard_map/reduce_scatter | solution.py:95
  165.4 3.9 %copy-start.3 = (bf16[1,2,352,2048]{3,2,1,0:T(8,128)(2,1)S(1)}, bf16[1,2,352,2048]{3,2,1,0:T(8,128)(2,1)}, u32[]{:S(2)}) copy-start(bf16[1,2,352,2048]{3,2,1,0:T(8,128)(2,1)} %param.12) | copy-start | bytes 8650756
  173.6 1.0 copy-start.5
  218.0 55.8 %all-to-all-start.1 = ((bf16[8,1,32,2048]{3,2,1,0:T(8,128)(2,1)}), bf16[8,1,32,2048]{3,2,1,0:T(8,128)(2,1)S(1)}, u32[]{:S(2)}, u32[]{:S(2)}) async-start(bf16[8,1,32,2048]{3,2,1,0:T(8,128)(2,1)} %bitcast.187), calls=%async_computation.2 | async-start | bytes 2097152 | tf_op jit(solution)/shard_map/all_to_all | solution.py:89
  222.6 5.1 %copy-start.7 = (bf16[32,1,32,352]{3,2,0,1:T(8,128)(2,1)S(1)}, bf16[32,1,32,352]{3,2,0,1:T(8,128)(2,1)}, u32[]{:S(2)}) copy-start(bf16[32,1,32,352]{3,2,0,1:T(8,128)(2,1)} %copy-done.6) | copy-start | bytes 2162692
  222.7 5.1 %copy-start.11 = (bf16[32,1,32,2048]{3,2,1,0:T(8,128)(2,1)S(1)}, bf16[32,1,32,2048]{3,2,1,0:T(8,128)(2,1)}, u32[]{:S(2)}) copy-start(bf16[32,1,32,2048]{3,2,1,0:T(8,128)(2,1)} %all-gather.3.cloned.1.call-done) | copy-start | bytes 12582916
  273.9 8.4 %copy-start.1 = (bf16[8,1,32,2048]{3,2,1,0:T(8,128)(2,1)}, bf16[8,1,32,2048]{3,2,1,0:T(8,128)(2,1)S(1)}, u32[]{:S(2)}) copy-start(bf16[8,1,32,2048]{3,2,1,0:T(8,128)(2,1)S(1)} %all-to-all-done.1) | copy-start | bytes 3145732
  273.9 31.3 %all-to-all-start.3 = ((bf16[8,1,32,2048]{3,2,1,0:T(8,128)(2,1)}), bf16[8,1,32,2048]{3,2,1,0:T(8,128)(2,1)}, u32[]{:S(2)}, u32[]{:S(2)}) async-start(bf16[8,1,32,2048]{3,2,1,0:T(8,128)(2,1)} %bitcast.186), calls=%async_computation.5 | async-start | bytes 2097152 | tf_op jit(solution)/shard_map/all_to_all | solution.py:98
  278.5 3.8 %copy-start.12 = (bf16[32,1,32,2048]{3,2,1,0:T(8,128)(2,1)S(1)}, bf16[32,1,32,2048]{3,2,1,0:T(8,128)(2,1)}, u32[]{:S(2)}) copy-start(bf16[32,1,32,2048]{3,2,1,0:T(8,128)(2,1)} %all-gather.5.cloned.1.call-done) | copy-start | bytes 12582916
  278.5 3.8 %copy-start.14 = (bf16[32,32,352]{2,1,0:T(8,128)(2,1)S(1)}, bf16[32,32,352]{2,1,0:T(8,128)(2,1)}, u32[]{:S(2)}) copy-start(bf16[32,32,352]{2,1,0:T(8,128)(2,1)} %copy-done.13) | copy-start | bytes 2162692
Sparse Core Ops, SparseCore 0:
  47.8 51.5 all-gather.2
  101.3 52.6 all-gather.4
  165.3 52.6 reduce-scatter.2
  221.1 52.6 reduce-scatter.4
where the time goes:
time: 321 us
  waiting for transfers between devices  155 us (48%)
  blocking collectives  62.5 us (19%)
  matrix products  39 us (12%)
  local copies, waits for them, and re-layouts  23.8 us (7%)
  other arithmetic  16.9 us (5%)
  between operations  14 us (4%)
  starting transfers between devices  9.58 us (3%)
    all_gather x1, waiting for transfers between devices, body(): use_scaled = lax.all_gather(recv_scaled, 'dp', axis=0, tiled=True)  44.7 us
    reduce_scatter x1, waiting for transfers between devices, body(): lax.psum_scatter(input_grad.astype(jnp.bfloat16), 'dp', scatter_dimension...  43.2 us
    reduce_scatter x1, waiting for transfers between devices, body(): lax.psum_scatter(partial_out.astype(jnp.bfloat16), 'dp', scatter_dimensio...  42.2 us
    all_to_all x1, blocking collectives, body(): lax.all_to_all(send_inputs, 'expert', split_axis=0, concat_axis=0, tiled=...  32.8 us
    all_to_all x1, blocking collectives, body(): lax.all_to_all(send_scaled, 'expert', split_axis=0, concat_axis=0, tiled=...  29.7 us
    all_gather x1, waiting for transfers between devices, body(): use_inputs = lax.all_gather(recv_inputs, 'dp', axis=0, tiled=True)  18 us
    all_to_all x1, waiting for transfers between devices, body(): lax.all_to_all(grad_local, 'expert', split_axis=0, concat_axis=0, tiled=T...  6.66 us
  transfers between devices with their start and end apart: 6, of which 5 were waited for; matrix products, arithmetic and copies ran while one was open for 16% of the time, Pallas kernels for 0%

commit v1 on v0

--- a/solution.py
+++ b/solution.py
@@ -1,7 +1,402 @@
+import functools
+
 import jax
 import jax.numpy as jnp
 from jax import lax
+from jax.experimental import pallas as pl
+from jax.experimental.pallas import tpu as pltpu
 from jax.sharding import PartitionSpec as P
+
+MESH = pl.DeviceIdType.MESH
+OWN, XN, DG, YN = 0, 1, 2, 3
+
+
+def flip(value, amount, bits):
+    out = 0
+    for b in range(bits):
+        w = 1 << b
+        out = out + ((value // w + amount // w) % 2) * w
+    return out
+
+
+def dot_nt(a, b):
+    return lax.dot_general(a, b, (((1,), (1,)), ((), ())), preferred_element_type=jnp.float32)
+
+
+def dot_nn(a, b):
+    return lax.dot_general(a, b, (((1,), (0,)), ((), ())), preferred_element_type=jnp.float32)
+
+
+def dot_tn(a, b):
+    return lax.dot_general(a, b, (((0,), (0,)), ((), ())), preferred_element_type=jnp.float32)
+
+
+def moe_kernel(
+    n, tok, cot, pick, rw_slot, comb, comb_hi, comb_lo, w_in, w_down,
+    mixed, d_tok, d_slot, d_in, d_down,
+    xb, cb, ob, gb, sx, sc, r1o, r1g, r2o, r2g, bo, bg,
+    wi, wd, gate, up, hid, gg, ug, dwi, dwd,
+    s_a, r_a, s_x, r_x, s_y, r_y, s_d, r_d, s_1, r_1, s_2, r_2, s_b, r_b, s_w,
+):
+    bits = n.bit_length() - 1
+    g = lax.axis_index("dp")
+    e = lax.axis_index("expert")
+    nx = {"dp": flip(g, 1, 2)}
+    ny = {"dp": flip(g, 2, 2)}
+    slots = xb.shape[2]
+    width = xb.shape[3]
+    ff = wd.shape[0]
+    rows = n * slots
+    half = n // 2
+    cw = width // 4
+    cols = [pl.ds(i * cw, cw) for i in range(4)]
+    bf = jnp.bfloat16
+    f32 = jnp.float32
+
+    def peer(d):
+        return {"expert": flip(e, d, bits)}
+
+    def rcopy(src, dst, s, r, dev):
+        return pltpu.make_async_remote_copy(
+            src_ref=src, dst_ref=dst, send_sem=s, recv_sem=r, device_id=dev, device_id_type=MESH
+        )
+
+    gather = ((sx, xb), (sc, cb))
+    reduce = ((ob, r1o, r2o, bo), (gb, r1g, r2g, bg))
+
+    def send_a(i, d):
+        s, b = gather[i]
+        return rcopy(s.at[d], b.at[OWN, d], s_a.at[i, d], r_a.at[i, d], peer(d))
+
+    def send_x(i, d):
+        b = gather[i][1]
+        return rcopy(b.at[OWN, d], b.at[XN, d], s_x.at[i, d], r_x.at[i, d], nx)
+
+    def send_y(i, d):
+        b = gather[i][1]
+        return rcopy(b.at[OWN, d], b.at[YN, d], s_y.at[i, d], r_y.at[i, d], ny)
+
+    def send_d(i, d, odd):
+        b = gather[i][1]
+        if odd:
+            return rcopy(b.at[YN, d], b.at[DG, d], s_d.at[i, d], r_d.at[i, d], nx)
+        return rcopy(b.at[XN, d], b.at[DG, d], s_d.at[i, d], r_d.at[i, d], ny)
+
+    def send_1(i, d, odd):
+        b, r1 = reduce[i][:2]
+        if odd:
+            return rcopy(b.at[pl.ds(DG, 2), d], r1.at[d], s_1.at[i, d], r_1.at[i, d], ny)
+        return rcopy(b.at[pl.ds(XN, 2), d], r1.at[d], s_1.at[i, d], r_1.at[i, d], nx)
+
+    def send_2(i, d, odd):
+        b, _, r2, _ = reduce[i]
+        if odd:
+            return rcopy(b.at[XN, d], r2.at[d], s_2.at[i, d], r_2.at[i, d], nx)
+        return rcopy(b.at[YN, d], r2.at[d], s_2.at[i, d], r_2.at[i, d], ny)
+
+    def send_b(i, d):
+        b, _, _, back = reduce[i]
+        return rcopy(b.at[OWN, d], back.at[d], s_b.at[i, d], r_b.at[i, d], peer(d))
+
+    def forward(i, d, odd):
+        (send_y if odd else send_x)(i, d).wait_recv()
+        send_d(i, d, odd).start()
+
+    def middle(i, d, odd):
+        b, r1 = reduce[i][:2]
+        send_1(i, d, odd).wait_recv()
+        at, got = (XN, 0) if odd else (YN, 1)
+        b[at, d] = (b[at, d].astype(f32) + r1[d, got].astype(f32)).astype(bf)
+        send_2(i, d, odd).start()
+
+    def finish(i, d, odd):
+        b, r1, r2, back = reduce[i]
+        send_2(i, d, odd).wait_recv()
+        got = 1 if odd else 0
+        total = b[OWN, d].astype(f32) + r1[d, got].astype(f32) + r2[d].astype(f32)
+        b[OWN, d] = total.astype(bf)
+
+    def load_w():
+        return (
+            pltpu.make_async_copy(w_in, wi, s_w.at[0]),
+            pltpu.make_async_copy(w_down, wd, s_w.at[1]),
+        )
+
+    def group_wait(i, pos):
+        if pos == XN:
+            for d in range(1, n, 2):
+                send_x(i, d).wait_recv()
+        if pos == YN:
+            for d in range(0, n, 2):
+                send_y(i, d).wait_recv()
+        if pos == DG:
+            for d in range(n):
+                send_d(i, d, d % 2).wait_recv()
+
+    barrier = pltpu.get_barrier_semaphore()
+    for d in range(1, n):
+        pl.semaphore_signal(barrier, inc=1, device_id=peer(d), device_id_type=MESH)
+    for dev in (nx, ny):
+        pl.semaphore_signal(barrier, inc=1, device_id=dev, device_id_type=MESH)
+    for c in load_w():
+        c.start()
+
+    def bucket(i, d):
+        at = pl.ds(d * slots, slots)
+        source = (tok, cot)[i]
+        for c in cols:
+            v = dot_nn(pick[at, :], source[:, c])
+            if i:
+                v = v * rw_slot[at, :]
+            gather[i][0][d, :, c] = v.astype(bf)
+
+    bucket(0, 0)
+    xb[OWN, 0] = sx[0]
+    pl.semaphore_wait(barrier, n + 1)
+    send_x(0, 0).start()
+    send_y(0, 0).start()
+
+    @pl.loop(1, n)
+    def _(d):
+        bucket(0, d)
+        send_a(0, d).start()
+
+    @pl.loop(0, n)
+    def _(d):
+        bucket(1, d)
+
+    cb[OWN, 0] = sc[0]
+
+    lag = 2
+    for k in range(n + lag):
+        if k < n:
+            if k:
+                send_a(0, k).wait_recv()
+                send_x(0, k).start()
+                send_y(0, k).start()
+                send_a(1, k).start()
+        if k >= lag:
+            forward(0, k - lag, (k - lag) % 2)
+
+    for c in load_w():
+        c.wait()
+
+    per = half // 4
+
+    def expert_fwd(q):
+        at = pl.ds(q * rows, rows)
+        x = xb[q].reshape(rows, width)
+        gv = dot_nt(x, wi[0])
+        uv = dot_nt(x, wi[1])
+        gate[at, :] = gv
+        up[at, :] = uv
+        h = (gv * jax.nn.sigmoid(gv) * uv).astype(bf)
+        hid[at, :] = h
+        for c in cols:
+            ob[q, :, :, c] = dot_nn(h, wd[:, c]).astype(bf).reshape(n, slots, cw)
+
+    def expert_bwd(q):
+        at = pl.ds(q * rows, rows)
+        hg = dot_nt(cb[q].reshape(rows, width), wd[...])
+        gv = gate[at, :]
+        uv = up[at, :]
+        sg = jax.nn.sigmoid(gv)
+        a = (hg * uv * (sg * (1.0 + gv * (1.0 - sg)))).astype(bf)
+        b = (hg * (gv * sg)).astype(bf)
+        gg[at, :] = a
+        ug[at, :] = b
+        for c in cols:
+            v = dot_nn(a, wi[0, :, c]) + dot_nn(b, wi[1, :, c])
+            gb[q, :, :, c] = v.astype(bf).reshape(n, slots, cw)
+
+    send_x(1, 0).start()
+    send_y(1, 0).start()
+
+    @pl.loop(0, 4)
+    def _(q):
+        for p in range(per):
+            for odd in (0, 1):
+                d = (q * per + p) * 2 + odd
+
+                @pl.when(d > 0)
+                def _():
+                    send_a(1, d).wait_recv()
+                    send_x(1, d).start()
+                    send_y(1, d).start()
+
+        @pl.when(q > 0)
+        def _():
+            for p in range(per):
+                for odd in (0, 1):
+                    forward(1, ((q - 1) * per + p) * 2 + odd, odd)
+
+        for pos in (XN, DG, YN):
+
+            @pl.when(q == pos)
+            def _():
+                group_wait(0, pos)
+
+        expert_fwd(q)
+
+    for d in range(n):
+        if d >= n - 2 * per:
+            forward(1, d, d % 2)
+        send_1(0, d, d % 2).start()
+
+    @pl.loop(0, 4)
+    def _(q):
+        for pos in (XN, DG, YN):
+
+            @pl.when(q == pos - 1)
+            def _():
+                group_wait(1, pos)
+
+        expert_bwd((q + 1) % 4)
+
+        @pl.when(q == 2)
+        def _():
+            for d in range(n):
+                send_1(1, d, d % 2).start()
+
+        for p in range(per):
+            for odd in (0, 1):
+                middle(0, (q * per + p) * 2 + odd, odd)
+
+    @pl.loop(0, 4)
+    def _(q):
+        c = pl.ds(pl.multiple_of(q * cw, cw), cw)
+        for p in range(per):
+            for odd in (0, 1):
+                d = (q * per + p) * 2 + odd
+                finish(0, d, odd)
+
+                @pl.when(d > 0)
+                def _():
+                    send_b(0, d).start()
+
+                middle(1, d, odd)
+        x = xb[:, :, :, c].reshape(4 * rows, cw)
+        dwi[0, :, c] = dot_tn(gg[...], x).astype(bf)
+        dwi[1, :, c] = dot_tn(ug[...], x).astype(bf)
+        dwd[:, c] = dot_tn(hid[...], cb[:, :, :, c].reshape(4 * rows, cw)).astype(bf)
+
+    def store_w():
+        return (
+            pltpu.make_async_copy(dwi, d_in, s_w.at[2]),
+            pltpu.make_async_copy(dwd, d_down, s_w.at[3]),
+        )
+
+    for c in store_w():
+        c.start()
+
+    @pl.loop(0, half)
+    def _(h):
+        for odd in (0, 1):
+            d = h * 2 + odd
+            finish(1, d, odd)
+
+            @pl.when(d > 0)
+            def _():
+                send_b(1, d).start()
+
+    bo[0] = ob[OWN, 0]
+    bg[0] = gb[OWN, 0]
+    for d in range(1, n):
+        send_b(0, d).wait_recv()
+    back = bo[...].reshape(rows, width)
+    acc = jnp.zeros((rows, 1), f32)
+    for c in cols:
+        part = back[:, c.start : c.start + cw]
+        mixed[:, c] = (dot_nn(comb_hi[...], part) + dot_nn(comb_lo[...], part)).astype(bf)
+        acc = acc + jnp.sum(part.astype(f32) * dot_nn(pick[...], cot[:, c]), axis=1, keepdims=True)
+    d_slot[...] = acc
+    for d in range(1, n):
+        send_b(1, d).wait_recv()
+    for c in cols:
+        d_tok[:, c] = dot_nn(comb[...], bg[:, :, c].reshape(rows, cw)).astype(bf)
+
+    for i in (0, 1):
+        for d in range(n):
+            if d:
+                send_a(i, d).wait_send()
+                send_b(i, d).wait_send()
+            send_x(i, d).wait_send()
+            send_y(i, d).wait_send()
+            send_d(i, d, d % 2).wait_send()
+            send_1(i, d, d % 2).wait_send()
+            send_2(i, d, d % 2).wait_send()
+    for c in store_w():
+        c.wait()
+
+
+def fused(tokens, cotangent, routes, route_weights, capacity, w_in, w_down):
+    n = capacity.shape[0]
+    tok_rows, width = tokens.shape
+    slots = tok_rows * 2 // n
+    ff = w_down.shape[1]
+    rows = n * slots
+    bf, f32, i32 = jnp.bfloat16, jnp.float32, jnp.int32
+    e = lax.axis_index("expert")
+    flat = routes.reshape(-1)
+    count = 2 * tok_rows
+    same = flat[:, None] == flat[None, :]
+    before = lax.broadcasted_iota(i32, (count, count), 1) < lax.broadcasted_iota(i32, (count, count), 0)
+    rank = jnp.sum((same & before).astype(i32), axis=1).reshape(tok_rows, 2)
+    row = lax.iota(i32, rows)
+    row_expert = e ^ (row // slots)
+    row_rank = row % slots
+    row_cap = jnp.sum(
+        jnp.where(row_expert[:, None] == lax.iota(i32, n)[None, :], capacity[None, :], 0), axis=1
+    )
+    row_ok = row_rank < row_cap
+    hit = (
+        (routes[:, :, None] == row_expert)
+        & (rank[:, :, None] == row_rank)
+        & row_ok
+    )
+    comb = (hit[:, 0] | hit[:, 1]).astype(bf)
+    pick = comb.T
+    weighted = jnp.sum(jnp.where(hit, route_weights[:, :, None], 0.0), axis=1)
+    comb_hi = weighted.astype(bf)
+    comb_lo = (weighted - comb_hi.astype(f32)).astype(bf)
+    rw_slot = jnp.sum(weighted, axis=0)[:, None]
+    vm = pl.BlockSpec(memory_space=pltpu.VMEM)
+    hbm = pl.BlockSpec(memory_space=pl.ANY)
+    big = pltpu.VMEM((4, n, slots, width), bf)
+    piece = pltpu.VMEM((n, slots, width), bf)
+    two = pltpu.VMEM((n, 2, slots, width), bf)
+    sem = pltpu.SemaphoreType.DMA((2, n))
+    mixed, d_tok, d_slot, d_in, d_down = pl.pallas_call(
+        functools.partial(moe_kernel, n),
+        out_shape=(
+            jax.ShapeDtypeStruct((tok_rows, width), bf),
+            jax.ShapeDtypeStruct((tok_rows, width), bf),
+            jax.ShapeDtypeStruct((rows, 1), f32),
+            jax.ShapeDtypeStruct((2, ff, width), bf),
+            jax.ShapeDtypeStruct((ff, width), bf),
+        ),
+        in_specs=[vm] * 7 + [hbm] * 2,
+        out_specs=(vm, vm, vm, hbm, hbm),
+        scratch_shapes=[
+            big, big, big, big, piece, piece, two, two, piece, piece, piece, piece,
+            pltpu.VMEM((2, ff, width), bf),
+            pltpu.VMEM((ff, width), bf),
+            pltpu.VMEM((4 * rows, ff), f32),
+            pltpu.VMEM((4 * rows, ff), f32),
+            pltpu.VMEM((4 * rows, ff), bf),
+            pltpu.VMEM((4 * rows, ff), bf),
+            pltpu.VMEM((4 * rows, ff), bf),
+            pltpu.VMEM((2, ff, width), bf),
+            pltpu.VMEM((ff, width), bf),
+        ]
+        + [sem] * 14
+        + [pltpu.SemaphoreType.DMA((4,))],
+        compiler_params=pltpu.CompilerParams(
+            collective_id=0, has_side_effects=True, vmem_limit_bytes=60 * 2**20
+        ),
+    )(tokens, cotangent, pick, rw_slot, comb, comb_hi, comb_lo, w_in[0], w_down[0])
+    d_rw = jnp.sum(jnp.where(hit, d_slot[:, 0], 0.0), axis=2)
+    return mixed, d_tok, d_rw, d_in[None], d_down[None]
 
 
 def expert_forward(inputs, weights_in, weights_down):
@@ -53,10 +448,15 @@
     tok_rows = tokens.shape[0]
     width = tokens.shape[1]
     slots = tok_rows * 2 // experts
+    power = experts & (experts - 1) == 0 and experts % 8 == 0
+    if local_experts == 1 and slots % 16 == 0 and power and lax.axis_size("dp") == 4:
+        return fused(tokens, cotangent, routes, route_weights, capacity, w_in, w_down)
     flat_expert = routes.reshape(-1)
     expert_ids = jnp.arange(experts, dtype=jnp.int32)
     onehot = (flat_expert[:, None] == expert_ids[None, :]).astype(jnp.int32)
-    earlier = jnp.cumsum(onehot, axis=0) - onehot
+    ids = jnp.arange(flat_expert.shape[0], dtype=jnp.int32)
+    before = (ids[None, :] < ids[:, None]).astype(jnp.float32)
+    earlier = jnp.dot(before, onehot.astype(jnp.float32)).astype(jnp.int32)
     route_rank = jnp.sum(earlier * onehot, axis=1)
     cap_limit = jnp.sum(onehot * capacity[None, :], axis=1)
     kept_mask = route_rank < cap_limit

time: 321 us -> 193 us (0.60)
  Pallas kernels: 0 us -> 173 us
  waiting for transfers between devices: 155 us -> 0 us
  blocking collectives: 62.5 us -> 0 us
  matrix products: 39 us -> 0 us
  between operations: 14 us -> 0.68 us
  local copies, waits for them, and re-layouts: 23.8 us -> 11.4 us
  other arithmetic: 16.9 us -> 4.86 us
  starting transfers between devices: 9.58 us -> 0 us
    pallas_call x0 -> x1, Pallas kernels: none -> 173 us  [fused(): pl.pallas_call(functools.partial(moe_kernel, n), out_shape=(jax.ShapeDtyp...]
    reduce_scatter x2 -> x0, waiting for transfers between devices: 85.4 us -> none  [the longest x1 43.2 us: body(): lax.psum_scatter(input_grad.astype(jnp.bfloat16), 'dp', scatter_dimension...]
    all_gather x2 -> x0, waiting for transfers between devices: 62.7 us -> none  [the longest x1 44.7 us: body(): use_scaled = lax.all_gather(recv_scaled, 'dp', axis=0, tiled=True)]
    all_to_all x2 -> x0, blocking collectives: 62.5 us -> none  [the longest x1 32.8 us: body(): lax.all_to_all(send_inputs, 'expert', split_axis=0, concat_axis=0, tiled=...]
    dot_general x9 -> x0, matrix products: 39 us -> none  [the longest x1 6.34 us: expert_forward(): jnp.einsum('gecd,ehd->gech', inputs, weights_in[:, 1], preferred_element_...]
    gather x5 -> x0, local copies, waits for them, and re-layouts: 9.31 us -> none  [the longest x1 2.32 us: body(): flat_out[slot_target].reshape(tok_rows, 2, width).astype(jnp.float32)]
    all_to_all x2 -> x0, starting transfers between devices: 9.23 us -> none  [the longest x1 4.63 us: body(): lax.all_to_all(out_local, 'expert', split_axis=0, concat_axis=0, tiled=True)]
    reduce_sum x3 -> x4, other arithmetic: 10.3 us -> 2.52 us  [the longest x1 0.91 us: fused(): weighted = jnp.sum(jnp.where(hit, route_weights[:, :, None], 0.0), axis=1)]
  transfers between devices with their start and end apart: 6 -> 0, of which waited for: 5 -> 0; matrix products, arithmetic and copies ran while one was open for 16% -> 0% of each run, Pallas kernels for 0% -> 0%
where the time goes in v1:
time: 193 us; the launch traced here: 190 us
  Pallas kernels  173 us (90%)
  local copies, waits for them, and re-layouts  11.4 us (6%)
  other arithmetic  4.86 us (3%)
    pallas_call x1, Pallas kernels, fused(): pl.pallas_call(functools.partial(moe_kernel, n), out_shape=(jax.ShapeDtyp...  173 us
    unnamed x7, local copies, waits for them, and re-layouts  9.52 us

profile of v1, /device:TPU:0, one launch (start us, length us, event | category | flops | bytes accessed | tf_op | source)
XLA Modules:
  0.0 189.6 jit_solution(801843464387004971)
XLA Ops:
  0.6 0.7 select_reduce_fusion.3
  1.4 0.8 copy.17
  2.2 0.1 eq.61
  2.3 0.2 convert_reduce_fusion
  2.5 0.1 eq.65
  2.7 0.1 copy.18
  2.7 0.9 select_reduce_fusion
  3.6 0.7 subtract_convert_fusion
  4.3 0.8 copy.20.rw_slot
  5.1 0.7 fusion.3
  5.7 0.7 copy.19.pick
  6.5 172.6 %shard_map.110 = (bf16[128,2048]{1,0:T(8,128)(2,1)}, bf16[128,2048]{1,0:T(8,128)(2,1)}, f32[256,1]{1,0:T(8,128)}, bf16[2,352,2048]{2,1,0:T(8,128)(2,1)}, bf16[352,2048]{1,0:T(8,128)(2,1)}) custom-call(bf16[128,2048]{1,0:T(8,128)(2,1)} %tok.1, bf16[128,2048]{1,0:T(8,128)(2,1)} %cot.1, bf16[256,128]{1,0:T(8,128)(2,1)} %copy.19.pick, f32[256,1]{1,0:T(8,128)} %copy.20.rw_slot, ...), custom_call_target="tpu_custom_call" | custom-call | tf_op jit(solution)/shard_map/pallas_call | solution.py:369
  179.1 1.0 reduce.1
  180.1 0.7 select_reduce_fusion.2
  180.8 1.9 copy.25
  182.7 1.9 copy.26
  184.6 0.0 copy-start
  184.6 3.9 %copy.27 = bf16[1,2,352,2048]{3,2,1,0:T(8,128)(2,1)} copy(bf16[1,2,352,2048]{3,2,1,0:T(8,128)(2,1)} %bitcast.11) | data formatting | bytes 5767168
  188.5 0.0 copy-done
  188.5 1.1 copy.28
  (2 shorter events, 0.0 us)
Async XLA Ops:
  184.6 3.9 %copy-start = (bf16[352,2048]{1,0:T(8,128)(2,1)S(1)}, bf16[352,2048]{1,0:T(8,128)(2,1)}, u32[]{:S(2)}) copy-start(bf16[352,2048]{1,0:T(8,128)(2,1)} %get-tuple-element.14) | copy-start | bytes 4325380

commit v2 on v1

--- a/solution.py
+++ b/solution.py
@@ -19,6 +19,14 @@
     return out
 
 
+def offset(d):
+    q = d // 2
+    low, high = q % 2, (q // 2) % 2
+    even = d - (q % 4) * 2 + 2 * (2 * ((low + high) % 2) + high)
+    odd = d % 2
+    return even * (1 - odd) + d * odd
+
+
 def dot_nt(a, b):
     return lax.dot_general(a, b, (((1,), (1,)), ((), ())), preferred_element_type=jnp.float32)
 
@@ -32,8 +40,9 @@
 
 
 def moe_kernel(
-    n, tok, cot, pick, rw_slot, comb, comb_hi, comb_lo, w_in, w_down,
-    mixed, d_tok, d_slot, d_in, d_down,
+    n, tok, cot, route, rw, cap, w_in, w_down,
+    mixed, d_tok, d_rw, d_in, d_down,
+    pick, first, comb_hi, comb_lo, rw_slot,
     xb, cb, ob, gb, sx, sc, r1o, r1g, r2o, r2g, bo, bg,
     wi, wd, gate, up, hid, gg, ug, dwi, dwd,
     s_a, r_a, s_x, r_x, s_y, r_y, s_d, r_d, s_1, r_1, s_2, r_2, s_b, r_b, s_w,
@@ -54,7 +63,7 @@
     f32 = jnp.float32
 
     def peer(d):
-        return {"expert": flip(e, d, bits)}
+        return {"expert": flip(e, offset(d), bits)}
 
     def rcopy(src, dst, s, r, dev):
         return pltpu.make_async_remote_copy(
@@ -150,38 +159,35 @@
                 v = v * rw_slot[at, :]
             gather[i][0][d, :, c] = v.astype(bf)
 
-    bucket(0, 0)
-    xb[OWN, 0] = sx[0]
-    pl.semaphore_wait(barrier, n + 1)
-    send_x(0, 0).start()
-    send_y(0, 0).start()
-
-    @pl.loop(1, n)
-    def _(d):
-        bucket(0, d)
-        send_a(0, d).start()
-
-    @pl.loop(0, n)
-    def _(d):
-        bucket(1, d)
-
-    cb[OWN, 0] = sc[0]
-
-    lag = 2
-    for k in range(n + lag):
-        if k < n:
-            if k:
-                send_a(0, k).wait_recv()
-                send_x(0, k).start()
-                send_y(0, k).start()
-                send_a(1, k).start()
-        if k >= lag:
-            forward(0, k - lag, (k - lag) % 2)
-
-    for c in load_w():
-        c.wait()
-
-    per = half // 4
+    toks = tok.shape[0]
+    expert = jnp.bitwise_xor(offset(lax.broadcasted_iota(jnp.int32, (n, toks), 0)), e)
+    m0 = route[0:1, :] == expert
+    m1 = route[1:2, :] == expert
+    limit = jnp.zeros((n, toks), jnp.int32)
+    for x in range(n):
+        limit = jnp.where(expert == x, cap[x], limit)
+    upper = jnp.where(
+        lax.broadcasted_iota(jnp.int32, (toks, toks), 0)
+        < lax.broadcasted_iota(jnp.int32, (toks, toks), 1),
+        1.0,
+        0.0,
+    ).astype(bf)
+    rank = dot_nn(jnp.where(m0 | m1, 1.0, 0.0).astype(bf), upper)
+    rank = jnp.where(rank < limit.astype(f32), rank, -1.0)
+    v0 = jnp.where(m0, rank, -1.0)
+    v1 = jnp.where(m1, rank, -1.0)
+    slot = lax.broadcasted_iota(jnp.int32, (slots, toks), 0).astype(f32)
+    for d in range(n):
+        at = pl.ds(d * slots, slots)
+        p0 = v0[d : d + 1, :] == slot
+        p1 = v1[d : d + 1, :] == slot
+        wt = jnp.where(p0, rw[0:1, :], 0.0) + jnp.where(p1, rw[1:2, :], 0.0)
+        hi = wt.astype(bf)
+        pick[at, :] = jnp.where(p0 | p1, 1.0, 0.0).astype(bf)
+        first[at, :] = jnp.where(p0, 1.0, 0.0)
+        comb_hi[at, :] = hi
+        comb_lo[at, :] = (wt - hi.astype(f32)).astype(bf)
+        rw_slot[at, :] = jnp.sum(wt, axis=1, keepdims=True)
 
     def expert_fwd(q):
         at = pl.ds(q * rows, rows)
@@ -209,111 +215,115 @@
             v = dot_nn(a, wi[0, :, c]) + dot_nn(b, wi[1, :, c])
             gb[q, :, :, c] = v.astype(bf).reshape(n, slots, cw)
 
-    send_x(1, 0).start()
-    send_y(1, 0).start()
-
-    @pl.loop(0, 4)
-    def _(q):
-        for p in range(per):
-            for odd in (0, 1):
-                d = (q * per + p) * 2 + odd
-
-                @pl.when(d > 0)
-                def _():
-                    send_a(1, d).wait_recv()
-                    send_x(1, d).start()
-                    send_y(1, d).start()
-
-        @pl.when(q > 0)
-        def _():
-            for p in range(per):
-                for odd in (0, 1):
-                    forward(1, ((q - 1) * per + p) * 2 + odd, odd)
-
-        for pos in (XN, DG, YN):
-
-            @pl.when(q == pos)
-            def _():
-                group_wait(0, pos)
-
-        expert_fwd(q)
-
-    for d in range(n):
-        if d >= n - 2 * per:
-            forward(1, d, d % 2)
-        send_1(0, d, d % 2).start()
-
-    @pl.loop(0, 4)
-    def _(q):
-        for pos in (XN, DG, YN):
-
-            @pl.when(q == pos - 1)
-            def _():
-                group_wait(1, pos)
-
-        expert_bwd((q + 1) % 4)
-
-        @pl.when(q == 2)
-        def _():
-            for d in range(n):
-                send_1(1, d, d % 2).start()
-
-        for p in range(per):
-            for odd in (0, 1):
-                middle(0, (q * per + p) * 2 + odd, odd)
-
-    @pl.loop(0, 4)
-    def _(q):
-        c = pl.ds(pl.multiple_of(q * cw, cw), cw)
-        for p in range(per):
-            for odd in (0, 1):
-                d = (q * per + p) * 2 + odd
-                finish(0, d, odd)
-
-                @pl.when(d > 0)
-                def _():
-                    send_b(0, d).start()
-
-                middle(1, d, odd)
-        x = xb[:, :, :, c].reshape(4 * rows, cw)
-        dwi[0, :, c] = dot_tn(gg[...], x).astype(bf)
-        dwi[1, :, c] = dot_tn(ug[...], x).astype(bf)
-        dwd[:, c] = dot_tn(hid[...], cb[:, :, :, c].reshape(4 * rows, cw)).astype(bf)
-
     def store_w():
         return (
             pltpu.make_async_copy(dwi, d_in, s_w.at[2]),
             pltpu.make_async_copy(dwd, d_down, s_w.at[3]),
         )
 
-    for c in store_w():
-        c.start()
-
-    @pl.loop(0, half)
-    def _(h):
-        for odd in (0, 1):
-            d = h * 2 + odd
-            finish(1, d, odd)
-
-            @pl.when(d > 0)
-            def _():
-                send_b(1, d).start()
-
-    bo[0] = ob[OWN, 0]
-    bg[0] = gb[OWN, 0]
-    for d in range(1, n):
-        send_b(0, d).wait_recv()
-    back = bo[...].reshape(rows, width)
-    acc = jnp.zeros((rows, 1), f32)
-    for c in cols:
-        part = back[:, c.start : c.start + cw]
-        mixed[:, c] = (dot_nn(comb_hi[...], part) + dot_nn(comb_lo[...], part)).astype(bf)
-        acc = acc + jnp.sum(part.astype(f32) * dot_nn(pick[...], cot[:, c]), axis=1, keepdims=True)
-    d_slot[...] = acc
-    for d in range(1, n):
-        send_b(1, d).wait_recv()
-    for c in cols:
-        d_tok[:, c] = dot_nn(comb[...], bg[:, :, c].reshape(rows, cw)).astype(bf)
+    def combine_out():
+        bo[0] = ob[OWN, 0]
+        for d in range(1, n):
+            send_b(0, d).wait_recv()
+        back = bo[...].reshape(rows, width)
+        acc = jnp.zeros((rows, 1), f32)
+        for c in cols:
+            part = back[:, c.start : c.start + cw]
+            mixed[:, c] = (dot_tn(comb_hi[...], part) + dot_tn(comb_lo[...], part)).astype(bf)
+            acc = acc + jnp.sum(part.astype(f32) * dot_nn(pick[...], cot[:, c]), axis=1, keepdims=True)
+        one = jnp.sum(acc * first[...], axis=0, keepdims=True)
+        d_rw[0:1, :] = one
+        d_rw[1:2, :] = jnp.sum(acc * (pick[...].astype(f32) - first[...]), axis=0, keepdims=True)
+    def combine_grad():
+        bg[0] = gb[OWN, 0]
+        for d in range(1, n):
+            send_b(1, d).wait_recv()
+        for c in cols:
+            d_tok[:, c] = dot_tn(pick[...], bg[:, :, c].reshape(rows, cw)).astype(bf)
+
+
+    def weight_grad(q):
+        c = cols[q]
+        x = xb[:, :, :, c].reshape(4 * rows, cw)
+        dwi[0, :, c] = dot_tn(gg[...], x).astype(bf)
+        dwi[1, :, c] = dot_tn(ug[...], x).astype(bf)
+        dwd[:, c] = dot_tn(hid[...], cb[:, :, :, c].reshape(4 * rows, cw)).astype(bf)
+
+    def scatter(i, d):
+        send_x(i, d).start()
+        send_y(i, d).start()
+
+    z_window, lag, r_window, r_lag = 4, 3, 2, 2
+    far = [(i, d) for i in (0, 1) for d in range(2, n)]
+    order = [(0, 1), (1, 1)] + far
+    spread = [(0, 0), (1, 0)] + order
+
+    bucket(0, 0)
+    xb[OWN, 0] = sx[0]
+    pl.semaphore_wait(barrier, n + 1)
+    scatter(0, 0)
+    for k, (i, d) in enumerate(order[:z_window]):
+        bucket(i, d)
+        send_a(i, d).start()
+        if k == 0:
+            bucket(1, 0)
+            cb[OWN, 0] = sc[0]
+            scatter(1, 0)
+    for c in load_w():
+        c.wait()
+
+    last = order.index((0, n - 1))
+    fwd_at = {last + 1: OWN, last + 3: XN, last + 4: YN, len(order) - 1: DG}
+    steps = len(order)
+    done = 0
+    for k in range(steps):
+        i, d = order[k]
+        send_a(i, d).wait_recv()
+        scatter(i, d)
+        if k + z_window < steps:
+            i, d = order[k + z_window]
+            bucket(i, d)
+            send_a(i, d).start()
+        if k + 2 - lag >= 0:
+            i, d = spread[k + 2 - lag]
+            forward(i, d, d % 2)
+            done = k + 3 - lag
+        if k in fwd_at:
+            group_wait(0, fwd_at[k])
+            expert_fwd(fwd_at[k])
+
+    chain = [(i, d) for i in (0, 1) for d in range(n - 1, -1, -1)]
+    for i, d in chain[:r_window]:
+        send_1(i, d, d % 2).start()
+    for i, d in spread[done:]:
+        forward(i, d, d % 2)
+
+    def close(i, d):
+        finish(i, d, d % 2)
+        if d:
+            send_b(i, d).start()
+
+    bwd_at = [XN, YN, DG, OWN]
+    for k in range(len(chain) + r_lag):
+        if k < 4:
+            group_wait(1, bwd_at[k])
+            expert_bwd(bwd_at[k])
+        if k < len(chain):
+            i, d = chain[k]
+            middle(i, d, d % 2)
+            if k + r_window < len(chain):
+                i, d = chain[k + r_window]
+                send_1(i, d, d % 2).start()
+        if k >= r_lag:
+            close(*chain[k - r_lag])
+        if 5 <= k < 9:
+            weight_grad(k - 5)
+        if k == 9:
+            for c in store_w():
+                c.start()
+        if k == len(chain) - 2:
+            combine_out()
+    combine_grad()
 
     for i in (0, 1):
         for d in range(n):
@@ -329,55 +339,76 @@
         c.wait()
 
 
+def land(*arrays):
+    cuts = []
+    for k, a in enumerate(arrays):
+        size = a.shape[-2]
+        parts = 2 if size % 32 == 0 else 1
+        for lead in range(a.shape[0] if a.ndim == 3 else 1):
+            for p in range(parts):
+                at = pl.ds(p * (size // parts), size // parts)
+                cuts.append((k, (lead, at) if a.ndim == 3 else (at,)))
+    m = len(arrays)
+
+    def run(*refs):
+        came, went = refs[-2:]
+        loads = [
+            pltpu.make_async_copy(refs[k].at[at], refs[2 * m + k].at[at], came.at[i])
+            for i, (k, at) in enumerate(cuts)
+        ]
+        stores = [
+            pltpu.make_async_copy(refs[2 * m + k].at[at], refs[m + k].at[at], went.at[i])
+            for i, (k, at) in enumerate(cuts)
+        ]
+        for c in loads:
+            c.start()
+        for a, b in zip(loads, stores):
+            a.wait()
+            b.start()
+        for c in stores:
+            c.wait()
+
+    return pl.pallas_call(
+        run,
+        out_shape=tuple(jax.ShapeDtypeStruct(a.shape, a.dtype) for a in arrays),
+        in_specs=[pl.BlockSpec(memory_space=pl.ANY)] * m,
+        out_specs=tuple([pl.BlockSpec(memory_space=pl.ANY)] * m),
+        scratch_shapes=[pltpu.VMEM(a.shape, a.dtype) for a in arrays]
+        + [pltpu.SemaphoreType.DMA((len(cuts),))] * 2,
+        compiler_params=pltpu.CompilerParams(vmem_limit_bytes=60 * 2**20),
+    )(*arrays)
+
+
 def fused(tokens, cotangent, routes, route_weights, capacity, w_in, w_down):
     n = capacity.shape[0]
     tok_rows, width = tokens.shape
     slots = tok_rows * 2 // n
     ff = w_down.shape[1]
     rows = n * slots
-    bf, f32, i32 = jnp.bfloat16, jnp.float32, jnp.int32
-    e = lax.axis_index("expert")
-    flat = routes.reshape(-1)
-    count = 2 * tok_rows
-    same = flat[:, None] == flat[None, :]
-    before = lax.broadcasted_iota(i32, (count, count), 1) < lax.broadcasted_iota(i32, (count, count), 0)
-    rank = jnp.sum((same & before).astype(i32), axis=1).reshape(tok_rows, 2)
-    row = lax.iota(i32, rows)
-    row_expert = e ^ (row // slots)
-    row_rank = row % slots
-    row_cap = jnp.sum(
-        jnp.where(row_expert[:, None] == lax.iota(i32, n)[None, :], capacity[None, :], 0), axis=1
-    )
-    row_ok = row_rank < row_cap
-    hit = (
-        (routes[:, :, None] == row_expert)
-        & (rank[:, :, None] == row_rank)
-        & row_ok
-    )
-    comb = (hit[:, 0] | hit[:, 1]).astype(bf)
-    pick = comb.T
-    weighted = jnp.sum(jnp.where(hit, route_weights[:, :, None], 0.0), axis=1)
-    comb_hi = weighted.astype(bf)
-    comb_lo = (weighted - comb_hi.astype(f32)).astype(bf)
-    rw_slot = jnp.sum(weighted, axis=0)[:, None]
+    bf, f32 = jnp.bfloat16, jnp.float32
     vm = pl.BlockSpec(memory_space=pltpu.VMEM)
     hbm = pl.BlockSpec(memory_space=pl.ANY)
     big = pltpu.VMEM((4, n, slots, width), bf)
     piece = pltpu.VMEM((n, slots, width), bf)
     two = pltpu.VMEM((n, 2, slots, width), bf)
     sem = pltpu.SemaphoreType.DMA((2, n))
-    mixed, d_tok, d_slot, d_in, d_down = pl.pallas_call(
+    mixed, d_tok, d_rw, d_in, d_down = pl.pallas_call(
         functools.partial(moe_kernel, n),
         out_shape=(
             jax.ShapeDtypeStruct((tok_rows, width), bf),
             jax.ShapeDtypeStruct((tok_rows, width), bf),
-            jax.ShapeDtypeStruct((rows, 1), f32),
+            jax.ShapeDtypeStruct((2, tok_rows), f32),
             jax.ShapeDtypeStruct((2, ff, width), bf),
             jax.ShapeDtypeStruct((ff, width), bf),
         ),
-        in_specs=[vm] * 7 + [hbm] * 2,
+        in_specs=[vm] * 4 + [pl.BlockSpec(memory_space=pltpu.SMEM)] + [hbm] * 2,
         out_specs=(vm, vm, vm, hbm, hbm),
         scratch_shapes=[
+            pltpu.VMEM((rows, tok_rows), bf),
+            pltpu.VMEM((rows, tok_rows), f32),
+            pltpu.VMEM((rows, tok_rows), bf),
+            pltpu.VMEM((rows, tok_rows), bf),
+            pltpu.VMEM((rows, 1), f32),
             big, big, big, big, piece, piece, two, two, piece, piece, piece, piece,
             pltpu.VMEM((2, ff, width), bf),
             pltpu.VMEM((ff, width), bf),
@@ -394,9 +425,9 @@
         compiler_params=pltpu.CompilerParams(
             collective_id=0, has_side_effects=True, vmem_limit_bytes=60 * 2**20
         ),
-    )(tokens, cotangent, pick, rw_slot, comb, comb_hi, comb_lo, w_in[0], w_down[0])
-    d_rw = jnp.sum(jnp.where(hit, d_slot[:, 0], 0.0), axis=2)
-    return mixed, d_tok, d_rw, d_in[None], d_down[None]
+    )(tokens, cotangent, routes.T, route_weights.T, capacity, w_in[0], w_down[0])
+    mixed, d_tok, d_in, d_down = land(mixed, d_tok, d_in, d_down)
+    return mixed, d_tok, d_rw.T, d_in[None], d_down[None]
 
 
 def expert_forward(inputs, weights_in, weights_down):

time: 193 us -> 158 us (0.82); the launches traced: 190 us -> 158 us
  Pallas kernels: 173 us -> 157 us
  local copies, waits for them, and re-layouts: 11.4 us -> 0.57 us
  other arithmetic: 4.86 us -> 0 us
    pallas_call x1, Pallas kernels: 173 us -> 152 us  [fused(): pl.pallas_call(functools.partial(moe_kernel, n), out_shape=(jax.ShapeDtyp...]
    unnamed x7 -> x3, local copies, waits for them, and re-layouts: 9.52 us -> 0.57 us
    pallas_call x0 -> x1, Pallas kernels: none -> 4.97 us  [land(): pl.pallas_call(run, out_shape=tuple((jax.ShapeDtypeStruct(a.shape, a.dtyp...]
    reduce_sum x4 -> x0, other arithmetic: 2.52 us -> none  [the longest x1 0.91 us: fused(): weighted = jnp.sum(jnp.where(hit, route_weights[:, :, None], 0.0), axis=1)]
where the time goes in v2:
time: 158 us
  Pallas kernels  157 us (99%)
    pallas_call x1, Pallas kernels, fused(): pl.pallas_call(functools.partial(moe_kernel, n), out_shape=(jax.ShapeDtyp...  152 us
    pallas_call x1, Pallas kernels, land(): pl.pallas_call(run, out_shape=tuple((jax.ShapeDtypeStruct(a.shape, a.dtyp...  4.97 us

profile of v2, /device:TPU:0, one launch (start us, length us, event | category | flops | bytes accessed | tf_op | source)
XLA Modules:
  0.0 157.8 jit_solution(63001755727723567)
XLA Ops:
  0.6 151.6 %shard_map.110 = (bf16[128,2048]{1,0:T(8,128)(2,1)}, bf16[128,2048]{1,0:T(8,128)(2,1)}, f32[2,128]{1,0:T(2,128)}, bf16[2,352,2048]{2,1,0:T(8,128)(2,1)}, bf16[352,2048]{1,0:T(8,128)(2,1)}) custom-call(bf16[128,2048]{1,0:T(8,128)(2,1)} %tok.1, bf16[128,2048]{1,0:T(8,128)(2,1)} %cot.1, s32[2,128]{1,0:T(2,128)} %bitcast.9, f32[2,128]{1,0:T(2,128)} %bitcast.10, ...), custom_call_target="tpu_custom_call" | custom-call | tf_op jit(solution)/shard_map/pallas_call | solution.py:395
  152.2 0.0 copy-start
  152.2 5.0 %shard_map.111 = (bf16[128,2048]{1,0:T(8,128)(2,1)}, bf16[128,2048]{1,0:T(8,128)(2,1)}, bf16[2,352,2048]{2,1,0:T(8,128)(2,1)}, bf16[352,2048]{1,0:T(8,128)(2,1)}) custom-call(bf16[128,2048]{1,0:T(8,128)(2,1)} %get-tuple-element.14.refs_0_, bf16[128,2048]{1,0:T(8,128)(2,1)} %get-tuple-element.15.refs_1_, bf16[2,352,2048]{2,1,0:T(8,128)(2,1)} %get-tuple-element.16.refs_2_, ...), custom_call_target="tpu_custom_call" | custom-call | tf_op jit(solution)/shard_map/pallas_call | solution.py:371
  157.2 0.0 copy-done
  157.2 0.6 copy.13
Async XLA Ops:
  152.2 5.0 %copy-start = (f32[2,128]{1,0:T(2,128)S(1)}, f32[2,128]{1,0:T(2,128)}, u32[]{:S(2)}) copy-start(f32[2,128]{1,0:T(2,128)} %get-tuple-element.20) | copy-start | bytes 3076
